TPU v7x, 512 devices: a whole 4x8x8 slice. The times are simulated.
512 devices in a mesh: vocab: 32 (over x, z), dp: 16 (over y, core).
Axes of the slice: x: 4, y: 8, z: 8, core: 2. Of those that a mesh axis runs over, the one named last changes fastest.
Arguments:
- out_grads: float32 [65536, 4096], P(('vocab', 'dp')), may hold values from -6 to 6
- token_ids: int32 [65536], P(('vocab', 'dp')), may hold values from 0 to 128255, as said below
Outputs:
- table_grad: bfloat16 [128256, 4096], P('vocab', 'dp')
Inputs may be any that keep to these rules, and one draw needn't show every extreme that they name: `token_ids`: call ids k * 4008 to (k + 1) * 4008 - 1 block k. The 128 tokens of one device hold at most 12 ids of any one block; one block, the same for all devices, holds exactly 12 ids of every device.
All inputs are finite; a program needn't handle non-finite values.
Results may differ from a plain program's by a relative error of at most 0.001.
Values sent between devices are 32-bit elements; how exact they have to be, the bound alone decides.
No kernel may reach another device: no remote copies, remote signals or barrier semaphores. Data moves between devices by JAX's collectives and lax.ppermute only.
A program may use at most 64 MiB of HBM per device.

v0:
```python
import jax
import jax.numpy as jnp
from jax import lax
from jax.sharding import PartitionSpec as P

VOCAB = 128256


def turned_gather(arrays, axis, dims):
    turned = [jnp.moveaxis(a, dim, 0) for a, dim in zip(arrays, dims)]
    both = jnp.concatenate([t.reshape(len(t), -1) for t in turned], axis=1)
    whole, at, outs = (lax.all_gather(both, axis, axis=0, tiled=True), 0, [])
    for t, dim in zip(turned, dims):
        share = whole[:, at : at + t[0].size].reshape(-1, *t.shape[1:])
        outs.append(jnp.moveaxis(share, 0, dim))
        at += t[0].size
    return tuple(outs)


def slot_tables(token_ids, rows_own, owners, capacity):
    tok_count = token_ids.shape[0]
    owner_of = token_ids // rows_own
    local_row = token_ids - owner_of * rows_own
    positions = lax.iota(jnp.int32, tok_count)
    earlier = (owner_of[:, None] == owner_of[None, :]) & (positions[None, :] < positions[:, None])
    slot_of = jnp.sum(earlier.astype(jnp.int32), axis=1)
    owner_ids = lax.iota(jnp.int32, owners)
    slot_ids = lax.iota(jnp.int32, capacity)
    matches = (owner_of[None, None, :] == owner_ids[:, None, None]) & (
        slot_of[None, None, :] == slot_ids[None, :, None]
    )
    filled = jnp.any(matches, axis=2)
    token_at = jnp.where(
        filled, jnp.sum(jnp.where(matches, positions[None, None, :], 0), axis=2), -1
    )
    row_at = jnp.where(filled, jnp.sum(jnp.where(matches, local_row[None, None, :], 0), axis=2), 0)
    return (token_at, row_at)


def local(out_grads, token_ids):
    owners = lax.axis_size("vocab")
    tok_count = token_ids.shape[0]
    rows_own = VOCAB // owners
    capacity = 3 * tok_count // owners
    token_at, row_at = slot_tables(token_ids, rows_own, owners, capacity)
    token_cols = lax.all_to_all(out_grads, "dp", split_axis=1, concat_axis=0, tiled=True)
    token_all, row_all = turned_gather((token_at, row_at), "dp", (1, 1))
    source = lax.broadcasted_iota(jnp.int32, token_all.shape, 1) // capacity
    index = source * tok_count + jnp.maximum(token_all, 0)
    picked = jnp.take(token_cols, index, axis=0)
    outgoing = jnp.where((token_all >= 0)[:, :, None], picked, 0.0)
    arrived, arrived_rows = (
        lax.all_to_all(outgoing, "vocab", split_axis=0, concat_axis=0, tiled=True),
        lax.all_to_all(row_all, "vocab", split_axis=0, concat_axis=0, tiled=True),
    )
    columns = arrived.reshape(-1, arrived.shape[2])
    row_index = arrived_rows.reshape(-1)
    table_sum = jax.ops.segment_sum(columns, row_index, num_segments=rows_own)
    return table_sum.astype(jnp.bfloat16)


def solution(mesh):
    in_specs = (P(("vocab", "dp"), None), P(("vocab", "dp")))
    out_specs = P("vocab", "dp")
    return jax.shard_map(local, mesh=mesh, in_specs=in_specs, out_specs=out_specs, check_vma=False)
```

profile of v0, /device:TPU:64, one launch (start us, length us, event | category | flops | bytes accessed | tf_op | source)
XLA Modules:
  0.0 306.3 jit_solution(15994949229476449633)
XLA Ops:
  0.0 0.0 copy-start
  0.0 3.2 %copy.28 = f32[16,16,8,256]{3,2,0,1:T(8,128)} copy(f32[16,16,8,256]{3,2,1,0:T(8,128)} %bitcast.29) | data formatting | bytes 4194304 | tf_op jit(solution)/shard_map/all_to_all | solution.py:46
  3.2 7.2 %all-to-all-start.1 = ((f32[128,16,256]{2,0,1:T(8,128)}), f32[128,16,256]{2,0,1:T(8,128)S(1)}, u32[]{:S(2)}, u32[]{:S(2)}) async-start(f32[128,16,256]{2,0,1:T(8,128)} %bitcast.28), calls=%async_computation.1 | async-start | bytes 4194304 | tf_op jit(solution)/shard_map/all_to_all | solution.py:46
  10.4 0.0 copy-done
  10.4 0.2 convert_reduce_fusion
  10.6 0.3 and_reduce_fusion
  10.9 0.5 fusion.2
  11.4 0.1 add_bitcast_fusion
  11.5 58.8 %all-gather = s32[16,12,64]{2,1,0:T(8,128)S(1)} all-gather(s32[1,12,64]{2,1,0:T(8,128)S(1)} %add_bitcast_fusion), channel_id=1, replica_groups=mesh['vocab'=32,'dp'=16] {'dp'}, dimensions={0}, use_global_device_ids=true | all-gather | bytes 52224 | tf_op jit(solution)/shard_map/all_gather | solution.py:12
  70.3 0.1 fusion.5
  70.4 0.1 copy.25
  70.5 0.1 reshape.67
  70.6 0.7 copy.22
  71.3 0.0 all-to-all-done.1
  71.3 12.6 %all-to-all-start = ((s32[32,1,192]{2,1,0:T(1,128)}), s32[32,1,192]{2,1,0:T(1,128)S(1)}, u32[]{:S(2)}, u32[]{:S(2)}) async-start(s32[32,1,192]{2,1,0:T(1,128)} %copy.22), calls=%async_computation | async-start | bytes 65536 | tf_op jit(solution)/shard_map/all_to_all | solution.py:54
  83.9 23.7 %gather_fusion = f32[6144,256]{1,0:T(8,128)} fusion(f32[2048,256]{1,0:T(8,128)S(1)} %bitcast.26, s32[6144]{0:T(1024)S(1)} %broadcast_clamp_fusion), kind=kCustom, calls=%fused_computation | custom fusion | bytes 12607488 | tf_op jit(solution)/shard_map/jit(_take)/gather | solution.py:50
  107.7 8.6 %select_select_fusion = f32[32,192,256]{2,1,0:T(8,128)} fusion(f32[32,192,256]{2,1,0:T(8,128)} %bitcast.27, pred[32,192]{1,0:T(8,128)(4,1)S(1)} %get-tuple-element.7, pred[32,192]{1,0:T(8,128)(4,1)S(1)} %compare_bitcast_fusion), kind=kLoop, calls=%fused_computation.2 | loop fusion | flops 3145728 | bytes 12595200 | tf_op jit(solution)/shard_map/jit(_where)/select_n | solution.py:51
  116.3 0.0 all-to-all-done
  116.3 9.8 %all-to-all-start.2 = ((f32[32,192,256]{2,1,0:T(8,128)}), f32[32,192,256]{2,1,0:T(8,128)}, u32[]{:S(2)}, u32[]{:S(2)}) async-start(f32[32,192,256]{2,1,0:T(8,128)} %select_select_fusion), calls=%async_computation.2 | async-start | bytes 12582912 | tf_op jit(solution)/shard_map/all_to_all | solution.py:53
  126.1 0.1 reduce
  126.2 0.1 reshape.75
  126.3 140.1 %all-to-all-done.2 = f32[32,192,256]{2,1,0:T(8,128)} async-done(((f32[32,192,256]{2,1,0:T(8,128)}), f32[32,192,256]{2,1,0:T(8,128)}, u32[]{:S(2)}, u32[]{:S(2)}) %all-to-all-start.2) | async-done | bytes 6291488 | tf_op jit(solution)/shard_map/all_to_all | solution.py:53
  266.4 36.2 %scatter_custom_fusion = f32[4008,256]{1,0:T(8,128)} fusion(s32[6144]{0:T(1024)S(1)} %reshape.75, f32[6144,256]{1,0:T(8,128)} %bitcast.10, f32[]{:T(128)} %constant.18.clone.1), kind=kCustom, calls=%fused_computation.4 | custom fusion | flops 1572864 | bytes 4104704 | tf_op jit(solution)/shard_map/scatter-add | solution.py:58
  302.7 3.7 %convert_element_type.7 = bf16[4008,256]{1,0:T(8,128)(2,1)} convert(f32[4008,256]{1,0:T(8,128)} %scatter_custom_fusion) | non-fusion elementwise | flops 1026048 | bytes 6156288 | tf_op jit(solution)/shard_map/convert_element_type | solution.py:59
  (10 shorter events, 0.1 us)
Async XLA Ops:
  0.0 10.4 %copy-start = (s32[128]{0:T(128)S(1)}, s32[128]{0:T(128)}, u32[]{:S(2)}) copy-start(s32[128]{0:T(128)} %param.3) | copy-start | bytes 1540
  3.2 68.1 %all-to-all-start.1 = ((f32[128,16,256]{2,0,1:T(8,128)}), f32[128,16,256]{2,0,1:T(8,128)S(1)}, u32[]{:S(2)}, u32[]{:S(2)}) async-start(f32[128,16,256]{2,0,1:T(8,128)} %bitcast.28), calls=%async_computation.1 | async-start | bytes 4194304 | tf_op jit(solution)/shard_map/all_to_all | solution.py:46
  71.3 45.0 %all-to-all-start = ((s32[32,1,192]{2,1,0:T(1,128)}), s32[32,1,192]{2,1,0:T(1,128)S(1)}, u32[]{:S(2)}, u32[]{:S(2)}) async-start(s32[32,1,192]{2,1,0:T(1,128)} %copy.22), calls=%async_computation | async-start | bytes 65536 | tf_op jit(solution)/shard_map/all_to_all | solution.py:54
  116.3 150.1 %all-to-all-start.2 = ((f32[32,192,256]{2,1,0:T(8,128)}), f32[32,192,256]{2,1,0:T(8,128)}, u32[]{:S(2)}, u32[]{:S(2)}) async-start(f32[32,192,256]{2,1,0:T(8,128)} %select_select_fusion), calls=%async_computation.2 | async-start | bytes 12582912 | tf_op jit(solution)/shard_map/all_to_all | solution.py:53
where the time goes:
time: 307 us; the launch traced here: 306 us
  waiting for transfers between devices  140 us (46%)
  blocking collectives  58.8 us (19%)
  other arithmetic  49.7 us (16%)
  starting transfers between devices  29.6 us (10%)
  local copies, waits for them, and re-layouts  27.9 us (9%)
    all_to_all x1, waiting for transfers between devices, local(): lax.all_to_all(outgoing, 'vocab', split_axis=0, concat_axis=0, tiled=True)  140 us
    all_gather x1, blocking collectives, turned_gather(): whole, at, outs = (lax.all_gather(both, axis, axis=0, tiled=True), 0, [])  58.8 us
    scatter-add x1, other arithmetic, local(): table_sum = jax.ops.segment_sum(columns, row_index, num_segments=rows_own)  36.2 us
    gather x1, local copies, waits for them, and re-layouts, local(): picked = jnp.take(token_cols, index, axis=0)  23.7 us
    all_to_all x1, starting transfers between devices, local(): lax.all_to_all(row_all, 'vocab', split_axis=0, concat_axis=0, tiled=True)  12.6 us
    all_to_all x1, starting transfers between devices, local(): lax.all_to_all(outgoing, 'vocab', split_axis=0, concat_axis=0, tiled=True)  9.84 us
    select_n x1, other arithmetic, local(): outgoing = jnp.where((token_all >= 0)[:, :, None], picked, 0.0)  8.62 us
    all_to_all x1, starting transfers between devices, local(): lax.all_to_all(out_grads, 'dp', split_axis=1, concat_axis=0, tiled=True)  7.21 us
  transfers between devices with their start and end apart: 3, of which 1 were waited for; matrix products, arithmetic and copies ran while one was open for 11% of the time, Pallas kernels for 0%

commit v1 on v0

--- a/solution.py
+++ b/solution.py
@@ -43,7 +43,10 @@
     rows_own = VOCAB // owners
     capacity = 3 * tok_count // owners
     token_at, row_at = slot_tables(token_ids, rows_own, owners, capacity)
-    token_cols = lax.all_to_all(out_grads, "dp", split_axis=1, concat_axis=0, tiled=True)
+    token_cols = jnp.concatenate(
+        lax.all_to_all(jnp.stack(jnp.split(out_grads, lax.axis_size("dp"), axis=1)), "dp", 0, 0),
+        axis=0,
+    )
     token_all, row_all = turned_gather((token_at, row_at), "dp", (1, 1))
     source = lax.broadcasted_iota(jnp.int32, token_all.shape, 1) // capacity
     index = source * tok_count + jnp.maximum(token_all, 0)

time: 307 us -> 329 us (1.072)
  local copies, waits for them, and re-layouts: 27.9 us -> 49.7 us
    unnamed x4 -> x19, local copies, waits for them, and re-layouts: 0.08 us -> 23.5 us
where the time goes in v1:
time: 329 us; the launch traced here: 328 us
  waiting for transfers between devices  140 us (43%)
  blocking collectives  58.8 us (18%)
  local copies, waits for them, and re-layouts  49.7 us (15%)
  other arithmetic  49.7 us (15%)
  starting transfers between devices  29.8 us (9%)
    all_to_all x1, waiting for transfers between devices, local(): lax.all_to_all(outgoing, 'vocab', split_axis=0, concat_axis=0, tiled=True)  140 us
    all_gather x1, blocking collectives, turned_gather(): whole, at, outs = (lax.all_gather(both, axis, axis=0, tiled=True), 0, [])  58.8 us
    scatter-add x1, other arithmetic, local(): table_sum = jax.ops.segment_sum(columns, row_index, num_segments=rows_own)  36.2 us
    gather x1, local copies, waits for them, and re-layouts, local(): picked = jnp.take(token_cols, index, axis=0)  23.7 us
    unnamed x19, local copies, waits for them, and re-layouts  23.5 us
    all_to_all x1, starting transfers between devices, local(): lax.all_to_all(row_all, 'vocab', split_axis=0, concat_axis=0, tiled=True)  12.6 us
    all_to_all x1, starting transfers between devices, local(): lax.all_to_all(outgoing, 'vocab', split_axis=0, concat_axis=0, tiled=True)  9.83 us
    select_n x1, other arithmetic, local(): outgoing = jnp.where((token_all >= 0)[:, :, None], picked, 0.0)  8.62 us
  transfers between devices with their start and end apart: 3, of which 1 were waited for; matrix products, arithmetic and copies ran while one was open for 11% of the time, Pallas kernels for 0%

profile of v1, /device:TPU:64, one launch (start us, length us, event | category | flops | bytes accessed | tf_op | source)
XLA Modules:
  0.0 328.3 jit_solution(6765984771206687894)
XLA Ops:
  0.0 1.5 bitcast_dynamic-update-slice_fusion.15
  1.6 1.6 bitcast_dynamic-update-slice_fusion.14
  3.1 1.6 bitcast_dynamic-update-slice_fusion.13
  4.7 1.6 bitcast_dynamic-update-slice_fusion.12
  6.2 1.6 bitcast_dynamic-update-slice_fusion.11
  9.4 1.6 bitcast_dynamic-update-slice_fusion.9
  10.9 1.6 bitcast_dynamic-update-slice_fusion.8
  12.5 1.6 bitcast_dynamic-update-slice_fusion.7
  14.1 1.6 bitcast_dynamic-update-slice_fusion.6
  15.6 1.6 bitcast_dynamic-update-slice_fusion.5
  17.2 1.6 bitcast_dynamic-update-slice_fusion.4
  18.7 1.6 bitcast_dynamic-update-slice_fusion.3
  20.3 1.6 bitcast_dynamic-update-slice_fusion.2
  21.9 1.6 bitcast_dynamic-update-slice_fusion.1
  23.4 1.6 bitcast_dynamic-update-slice_fusion
  25.0 7.3 %all-to-all-start.1 = ((f32[16,128,256]{2,1,0:T(8,128)}), f32[16,128,256]{2,1,0:T(8,128)S(1)}, u32[]{:S(2)}, u32[]{:S(2)}) async-start(f32[16,128,256]{2,1,0:T(8,128)} %bitcast_dynamic-update-slice_fusion), calls=%async_computation.1 | async-start | bytes 4194304 | tf_op jit(solution)/shard_map/all_to_all | solution.py:47
  33.4 58.8 %all-gather = s32[16,12,64]{2,1,0:T(8,128)S(1)} all-gather(s32[1,12,64]{2,1,0:T(8,128)S(1)} %add_bitcast_fusion), channel_id=1, replica_groups=mesh['vocab'=32,'dp'=16] {'dp'}, dimensions={0}, use_global_device_ids=true | all-gather | bytes 52224 | tf_op jit(solution)/shard_map/all_gather | solution.py:12
  93.2 12.6 %all-to-all-start = ((s32[32,1,192]{2,1,0:T(1,128)}), s32[32,1,192]{2,1,0:T(1,128)S(1)}, u32[]{:S(2)}, u32[]{:S(2)}) async-start(s32[32,1,192]{2,1,0:T(1,128)} %copy.17), calls=%async_computation | async-start | bytes 65536 | tf_op jit(solution)/shard_map/all_to_all | solution.py:57
  105.8 23.7 %gather_fusion = f32[6144,256]{1,0:T(8,128)} fusion(f32[2048,256]{1,0:T(8,128)S(1)} %bitcast.52, s32[6144]{0:T(1024)S(1)} %broadcast_clamp_fusion), kind=kCustom, calls=%fused_computation | custom fusion | bytes 12607488 | tf_op jit(solution)/shard_map/jit(_take)/gather | solution.py:53
  129.6 8.6 %select_select_fusion = f32[32,192,256]{2,1,0:T(8,128)} fusion(f32[32,192,256]{2,1,0:T(8,128)} %bitcast.53, pred[32,192]{1,0:T(8,128)(4,1)S(1)} %get-tuple-element.7, pred[32,192]{1,0:T(8,128)(4,1)S(1)} %compare_bitcast_fusion), kind=kLoop, calls=%fused_computation.2 | loop fusion | flops 3145728 | bytes 12595200 | tf_op jit(solution)/shard_map/jit(_where)/select_n | solution.py:54
  138.2 9.8 %all-to-all-start.2 = ((f32[32,192,256]{2,1,0:T(8,128)}), f32[32,192,256]{2,1,0:T(8,128)}, u32[]{:S(2)}, u32[]{:S(2)}) async-start(f32[32,192,256]{2,1,0:T(8,128)} %select_select_fusion), calls=%async_computation.2 | async-start | bytes 12582912 | tf_op jit(solution)/shard_map/all_to_all | solution.py:56
  148.2 140.1 %all-to-all-done.2 = f32[32,192,256]{2,1,0:T(8,128)} async-done(((f32[32,192,256]{2,1,0:T(8,128)}), f32[32,192,256]{2,1,0:T(8,128)}, u32[]{:S(2)}, u32[]{:S(2)}) %all-to-all-start.2) | async-done | bytes 6291488 | tf_op jit(solution)/shard_map/all_to_all | solution.py:56
  288.4 36.2 %scatter_custom_fusion = f32[4008,256]{1,0:T(8,128)} fusion(s32[6144]{0:T(1024)S(1)} %reshape.76, f32[6144,256]{1,0:T(8,128)} %bitcast.25, f32[]{:T(128)} %constant.18.clone.1), kind=kCustom, calls=%fused_computation.3 | custom fusion | flops 1572864 | bytes 4104704 | tf_op jit(solution)/shard_map/scatter-add | solution.py:61
  324.6 3.7 %convert_element_type.7 = bf16[4008,256]{1,0:T(8,128)(2,1)} convert(f32[4008,256]{1,0:T(8,128)} %scatter_custom_fusion) | non-fusion elementwise | flops 1026048 | bytes 6156288 | tf_op jit(solution)/shard_map/convert_element_type | solution.py:62
  (25 shorter events, 3.8 us)
Async XLA Ops:
  25.0 7.3 %copy-start = (s32[128]{0:T(128)S(1)}, s32[128]{0:T(128)}, u32[]{:S(2)}) copy-start(s32[128]{0:T(128)} %param.3) | copy-start | bytes 1540
  25.0 68.3 %all-to-all-start.1 = ((f32[16,128,256]{2,1,0:T(8,128)}), f32[16,128,256]{2,1,0:T(8,128)S(1)}, u32[]{:S(2)}, u32[]{:S(2)}) async-start(f32[16,128,256]{2,1,0:T(8,128)} %bitcast_dynamic-update-slice_fusion), calls=%async_computation.1 | async-start | bytes 4194304 | tf_op jit(solution)/shard_map/all_to_all | solution.py:47
  93.2 45.0 %all-to-all-start = ((s32[32,1,192]{2,1,0:T(1,128)}), s32[32,1,192]{2,1,0:T(1,128)S(1)}, u32[]{:S(2)}, u32[]{:S(2)}) async-start(s32[32,1,192]{2,1,0:T(1,128)} %copy.17), calls=%async_computation | async-start | bytes 65536 | tf_op jit(solution)/shard_map/all_to_all | solution.py:57
  138.2 150.1 %all-to-all-start.2 = ((f32[32,192,256]{2,1,0:T(8,128)}), f32[32,192,256]{2,1,0:T(8,128)}, u32[]{:S(2)}, u32[]{:S(2)}) async-start(f32[32,192,256]{2,1,0:T(8,128)} %select_select_fusion), calls=%async_computation.2 | async-start | bytes 12582912 | tf_op jit(solution)/shard_map/all_to_all | solution.py:56

commit v2 on v0

--- a/solution.py
+++ b/solution.py
@@ -9,7 +9,13 @@
 def turned_gather(arrays, axis, dims):
     turned = [jnp.moveaxis(a, dim, 0) for a, dim in zip(arrays, dims)]
     both = jnp.concatenate([t.reshape(len(t), -1) for t in turned], axis=1)
-    whole, at, outs = (lax.all_gather(both, axis, axis=0, tiled=True), 0, [])
+    whole, at, outs = (
+        jnp.concatenate(
+            lax.all_to_all(jnp.stack([both] * lax.axis_size(axis)), axis, 0, 0), axis=0
+        ),
+        0,
+        [],
+    )
     for t, dim in zip(turned, dims):
         share = whole[:, at : at + t[0].size].reshape(-1, *t.shape[1:])
         outs.append(jnp.moveaxis(share, 0, dim))

time: 307 us -> 306 us (level)
  blocking collectives: 58.8 us -> 0 us
  waiting for transfers between devices: 140 us -> 192 us
  starting transfers between devices: 29.6 us -> 33.3 us
    all_gather x1 -> x0, blocking collectives: 58.8 us -> none  [turned_gather(): whole, at, outs = (lax.all_gather(both, axis, axis=0, tiled=True), 0, [])]
    all_to_all x1, waiting for transfers between devices: 0.01 us -> 46.8 us  [local(): lax.all_to_all(out_grads, 'dp', split_axis=1, concat_axis=0, tiled=True)]
    all_to_all x0 -> x1, starting transfers between devices: none -> 7.21 us  [turned_gather(): lax.all_to_all(jnp.stack([both] * lax.axis_size(axis)), axis, 0, 0)]
    all_to_all x0 -> x1, waiting for transfers between devices: none -> 4.57 us  [turned_gather(): lax.all_to_all(jnp.stack([both] * lax.axis_size(axis)), axis, 0, 0)]
    all_to_all x1, starting transfers between devices: 7.21 us -> 3.72 us  [local(): lax.all_to_all(out_grads, 'dp', split_axis=1, concat_axis=0, tiled=True)]
  transfers between devices with their start and end apart: 3 -> 4, of which waited for: 1 -> 3; matrix products, arithmetic and copies ran while one was open for 11% -> 12% of each run, Pallas kernels for 0% -> 0%
where the time goes in v2:
time: 306 us; the launch traced here: 305 us
  waiting for transfers between devices  192 us (63%)
  other arithmetic  51.1 us (17%)
  starting transfers between devices  33.3 us (11%)
  local copies, waits for them, and re-layouts  29.3 us (10%)
    all_to_all x1, waiting for transfers between devices, local(): lax.all_to_all(outgoing, 'vocab', split_axis=0, concat_axis=0, tiled=True)  140 us
    all_to_all x1, waiting for transfers between devices, local(): lax.all_to_all(out_grads, 'dp', split_axis=1, concat_axis=0, tiled=True)  46.8 us
    scatter-add x1, other arithmetic, local(): table_sum = jax.ops.segment_sum(columns, row_index, num_segments=rows_own)  36.2 us
    gather x1, local copies, waits for them, and re-layouts, local(): picked = jnp.take(token_cols, index, axis=0)  23.7 us
    all_to_all x1, starting transfers between devices, local(): lax.all_to_all(row_all, 'vocab', split_axis=0, concat_axis=0, tiled=True)  12.6 us
    all_to_all x1, starting transfers between devices, local(): lax.all_to_all(outgoing, 'vocab', split_axis=0, concat_axis=0, tiled=True)  9.83 us
    select_n x1, other arithmetic, local(): outgoing = jnp.where((token_all >= 0)[:, :, None], picked, 0.0)  8.62 us
    all_to_all x1, starting transfers between devices, turned_gather(): lax.all_to_all(jnp.stack([both] * lax.axis_size(axis)), axis, 0, 0)  7.21 us
  transfers between devices with their start and end apart: 4, of which 3 were waited for; matrix products, arithmetic and copies ran while one was open for 12% of the time, Pallas kernels for 0%

profile of v2, /device:TPU:64, one launch (start us, length us, event | category | flops | bytes accessed | tf_op | source)
XLA Modules:
  0.0 305.4 jit_solution(8045604549020845272)
XLA Ops:
  0.0 0.7 multiply_subtract_fusion
  0.7 0.2 convert_reduce_fusion
  0.9 0.3 and_reduce_fusion
  1.2 0.5 fusion.2
  1.8 0.7 reshape.93
  2.5 7.2 %all-to-all-start = ((s32[16,1,768]{2,1,0:T(1,128)}), s32[16,1,768]{2,1,0:T(1,128)S(1)}, u32[]{:S(2)}, u32[]{:S(2)}) async-start(s32[16,1,768]{2,1,0:T(1,128)} %reshape.93), calls=%async_computation | async-start | bytes 98304 | tf_op jit(solution)/shard_map/all_to_all | solution.py:14
  9.7 3.2 %copy.28 = f32[16,16,8,256]{3,2,0,1:T(8,128)} copy(f32[16,16,8,256]{3,2,1,0:T(8,128)} %bitcast.27) | data formatting | bytes 4194304 | tf_op jit(solution)/shard_map/all_to_all | solution.py:52
  12.9 4.6 %all-to-all-done = s32[16,1,768]{2,1,0:T(1,128)S(1)} async-done(((s32[16,1,768]{2,1,0:T(1,128)}), s32[16,1,768]{2,1,0:T(1,128)S(1)}, u32[]{:S(2)}, u32[]{:S(2)}) %all-to-all-start) | async-done | bytes 49184 | tf_op jit(solution)/shard_map/all_to_all | solution.py:14
  17.4 3.7 %all-to-all-start.2 = ((f32[128,16,256]{2,0,1:T(8,128)}), f32[128,16,256]{2,0,1:T(8,128)S(1)}, u32[]{:S(2)}, u32[]{:S(2)}) async-start(f32[128,16,256]{2,0,1:T(8,128)} %bitcast.26), calls=%async_computation.2 | async-start | bytes 4194304 | tf_op jit(solution)/shard_map/all_to_all | solution.py:52
  21.2 0.5 broadcast.86
  21.7 0.8 reduce.1
  22.5 0.1 reshape.94
  22.6 0.1 fusion.5
  22.8 0.1 reshape.73
  22.9 0.7 copy.22
  23.6 46.8 %all-to-all-done.2 = f32[128,16,256]{2,0,1:T(8,128)S(1)} async-done(((f32[128,16,256]{2,0,1:T(8,128)}), f32[128,16,256]{2,0,1:T(8,128)S(1)}, u32[]{:S(2)}, u32[]{:S(2)}) %all-to-all-start.2) | async-done | bytes 2097184 | tf_op jit(solution)/shard_map/all_to_all | solution.py:52
  70.3 12.6 %all-to-all-start.1 = ((s32[32,1,192]{2,1,0:T(1,128)}), s32[32,1,192]{2,1,0:T(1,128)S(1)}, u32[]{:S(2)}, u32[]{:S(2)}) async-start(s32[32,1,192]{2,1,0:T(1,128)} %copy.22), calls=%async_computation.1 | async-start | bytes 65536 | tf_op jit(solution)/shard_map/all_to_all | solution.py:60
  82.9 23.7 %gather_fusion = f32[6144,256]{1,0:T(8,128)} fusion(f32[2048,256]{1,0:T(8,128)S(1)} %bitcast.24, s32[6144]{0:T(1024)S(1)} %broadcast_clamp_fusion), kind=kCustom, calls=%fused_computation | custom fusion | bytes 12607488 | tf_op jit(solution)/shard_map/jit(_take)/gather | solution.py:56
  106.7 8.6 %select_select_fusion = f32[32,192,256]{2,1,0:T(8,128)} fusion(f32[32,192,256]{2,1,0:T(8,128)} %bitcast.25, pred[32,192]{1,0:T(8,128)(4,1)S(1)} %get-tuple-element.7, pred[32,192]{1,0:T(8,128)(4,1)S(1)} %compare_bitcast_fusion), kind=kLoop, calls=%fused_computation.2 | loop fusion | flops 3145728 | bytes 12595200 | tf_op jit(solution)/shard_map/jit(_where)/select_n | solution.py:57
  115.3 9.8 %all-to-all-start.3 = ((f32[32,192,256]{2,1,0:T(8,128)}), f32[32,192,256]{2,1,0:T(8,128)}, u32[]{:S(2)}, u32[]{:S(2)}) async-start(f32[32,192,256]{2,1,0:T(8,128)} %select_select_fusion), calls=%async_computation.3 | async-start | bytes 12582912 | tf_op jit(solution)/shard_map/all_to_all | solution.py:59
  125.2 0.1 reshape.81
  125.3 140.2 %all-to-all-done.3 = f32[32,192,256]{2,1,0:T(8,128)} async-done(((f32[32,192,256]{2,1,0:T(8,128)}), f32[32,192,256]{2,1,0:T(8,128)}, u32[]{:S(2)}, u32[]{:S(2)}) %all-to-all-start.3) | async-done | bytes 6291488 | tf_op jit(solution)/shard_map/all_to_all | solution.py:59
  265.5 36.2 %scatter_custom_fusion = f32[4008,256]{1,0:T(8,128)} fusion(s32[6144]{0:T(1024)S(1)} %reshape.81, f32[6144,256]{1,0:T(8,128)} %bitcast.9, f32[]{:T(128)} %constant.18.clone.1), kind=kCustom, calls=%fused_computation.4 | custom fusion | flops 1572864 | bytes 4104704 | tf_op jit(solution)/shard_map/scatter-add | solution.py:64
  301.8 3.7 %convert_element_type.7 = bf16[4008,256]{1,0:T(8,128)(2,1)} convert(f32[4008,256]{1,0:T(8,128)} %scatter_custom_fusion) | non-fusion elementwise | flops 1026048 | bytes 6156288 | tf_op jit(solution)/shard_map/convert_element_type | solution.py:65
  (14 shorter events, 0.3 us)
Async XLA Ops:
  2.5 15.0 %all-to-all-start = ((s32[16,1,768]{2,1,0:T(1,128)}), s32[16,1,768]{2,1,0:T(1,128)S(1)}, u32[]{:S(2)}, u32[]{:S(2)}) async-start(s32[16,1,768]{2,1,0:T(1,128)} %reshape.93), calls=%async_computation | async-start | bytes 98304 | tf_op jit(solution)/shard_map/all_to_all | solution.py:14
  17.4 52.9 %all-to-all-start.2 = ((f32[128,16,256]{2,0,1:T(8,128)}), f32[128,16,256]{2,0,1:T(8,128)S(1)}, u32[]{:S(2)}, u32[]{:S(2)}) async-start(f32[128,16,256]{2,0,1:T(8,128)} %bitcast.26), calls=%async_computation.2 | async-start | bytes 4194304 | tf_op jit(solution)/shard_map/all_to_all | solution.py:52
  70.3 45.0 %all-to-all-start.1 = ((s32[32,1,192]{2,1,0:T(1,128)}), s32[32,1,192]{2,1,0:T(1,128)S(1)}, u32[]{:S(2)}, u32[]{:S(2)}) async-start(s32[32,1,192]{2,1,0:T(1,128)} %copy.22), calls=%async_computation.1 | async-start | bytes 65536 | tf_op jit(solution)/shard_map/all_to_all | solution.py:60
  115.3 150.3 %all-to-all-start.3 = ((f32[32,192,256]{2,1,0:T(8,128)}), f32[32,192,256]{2,1,0:T(8,128)}, u32[]{:S(2)}, u32[]{:S(2)}) async-start(f32[32,192,256]{2,1,0:T(8,128)} %select_select_fusion), calls=%async_computation.3 | async-start | bytes 12582912 | tf_op jit(solution)/shard_map/all_to_all | solution.py:59
